TPU v7x, 32 devices: a whole 2x2x4 slice. The times are simulated.
32 devices in a mesh: dp: 8 (over z, x), tensor: 4 (over y, core).
Axes of the slice: x: 2, y: 2, z: 4, core: 2. Of those that a mesh axis runs over, the one named last changes fastest.
Arguments:
- layer_input: bfloat16 [16384, 1536], P(('dp', 'tensor')), may hold values from -6 to 6
- out_grad: bfloat16 [16384, 1536], P(('dp', 'tensor')), may hold values from -6 to 6
- small_params: float32 [21392], replicated, may hold values from -7 to 3, as said below
- small_first: float32 [21392], replicated, as said below
- small_second: float32 [21392], replicated, may hold values from 862 to 3449
- w_zx: float32 [1536, 2, 3072], P('dp', None, 'tensor'), may hold values from -1 to 1, as said below
- zx_first: float32 [1536, 2, 3072], P('dp', None, 'tensor'), as said below
- zx_second: float32 [1536, 2, 3072], P('dp', None, 'tensor'), may hold values from 215 to 862
- w_bc: float32 [1536, 256], P('dp'), may hold values from -0.15625 to 0.15625
- bc_first: float32 [1536, 256], P('dp'), as said below
- bc_second: float32 [1536, 256], P('dp'), may hold values from 862 to 3449
- w_dt: float32 [1536, 48], P('dp', 'tensor'), may hold values from -0.15625 to 0.15625
- dt_first: float32 [1536, 48], P('dp', 'tensor'), as said below
- dt_second: float32 [1536, 48], P('dp', 'tensor'), may hold values from 862 to 3449
- w_out: float32 [1536, 3072], P('dp', 'tensor'), may hold values from -0.109375 to 0.109375
- out_first: float32 [1536, 3072], P('dp', 'tensor'), as said below
- out_second: float32 [1536, 3072], P('dp', 'tensor'), may hold values from 862 to 3449
Outputs:
- layer_output: bfloat16 [16384, 1536], P(('dp', 'tensor'))
- input_grad: float32 [16384, 1536], P(('dp', 'tensor'))
- small_new: float32 [21392], replicated
- small_first_new: float32 [21392], replicated
- small_second_new: float32 [21392], replicated
- zx_new: float32 [1536, 2, 3072], P('dp', None, 'tensor')
- zx_first_new: float32 [1536, 2, 3072], P('dp', None, 'tensor')
- zx_second_new: float32 [1536, 2, 3072], P('dp', None, 'tensor')
- bc_new: float32 [1536, 256], P('dp')
- bc_first_new: float32 [1536, 256], P('dp')
- bc_second_new: float32 [1536, 256], P('dp')
- dt_new: float32 [1536, 48], P('dp', 'tensor')
- dt_first_new: float32 [1536, 48], P('dp', 'tensor')
- dt_second_new: float32 [1536, 48], P('dp', 'tensor')
- out_new: float32 [1536, 3072], P('dp', 'tensor')
- out_first_new: float32 [1536, 3072], P('dp', 'tensor')
- out_second_new: float32 [1536, 3072], P('dp', 'tensor')
Inputs may be any that keep to these rules, and one draw needn't show every extreme that they name: `small_params`: gains near 1, convolution entries and biases within -0.5 to 0.5, softplus(dt_bias) within 0.001 to 0.1, exp(a_log) within 1 to 16, d_skip within 0.5 to 1.5. `small_first`: entries of both signs. `w_zx`: entries of order 1536 ** -0.5. `zx_first`: entries of both signs. `bc_first`: entries of both signs. `dt_first`: entries of both signs. `out_first`: entries of both signs.
All inputs are finite; a program needn't handle non-finite values.
Results may differ from a plain program's by a relative error of at most 0.0087.
The roundings to bfloat16 on the way count: a program that leaves them out, or rounds other values in their place, can miss the bound.
Values may be sent and summed in bfloat16 or wider, within the bound.
A program may use at most 256 MiB of HBM per device.

v0:
```python
import functools

import jax
import jax.numpy as jnp
from jax import lax
from jax.experimental import pallas as pl
from jax.experimental.pallas import tpu as pltpu
from jax.sharding import PartitionSpec as P

D = 1536
DI = 3072
H = 48
NS = 128
P_SIZE = 64
CONV = 4
LEN = 2048
STEP = 10

T = 128
ROWS = 256
LANES = 128
ROOM = 60 * 2**20

norm_eps = 1e-05
adam_eps = 1e-08
beta_first = 0.9
beta_second = 0.95
matrix_rate = 0.01
small_rate = 0.1
matrix_decay = 0.1

f32 = jnp.float32
bf16 = jnp.bfloat16
NN = (((1,), (0,)), ((), ()))
NT = (((1,), (1,)), ((), ()))
TN = (((0,), (0,)), ((), ()))
HIGHEST = lax.Precision.HIGHEST


GATE_ROW, TAPS_ROW, BIAS_ROW, TAPS_BC_ROW, BIAS_BC_ROW, HEAD_ROW, FLAT_ROWS = 12, 36, 132, 156, 164, 166, 168


def mm(a, b, dims=NN):
    return lax.dot_general(a, b, dims, preferred_element_type=f32)


def mm_exact(a, b, dims=NN):
    return lax.dot_general(a, b, dims, preferred_element_type=f32, precision=HIGHEST)


def sigmoid(v):
    return 0.5 * jnp.tanh(0.5 * v) + 0.5


def softplus(v):
    return jnp.maximum(v, 0.0) + jnp.log1p(jnp.exp(-jnp.abs(v)))


def spread(col):
    return jnp.broadcast_to(col, (T, LANES))


def block_iota(axis):
    return lax.broadcasted_iota(jnp.int32, (T, LANES), axis)


HEADS = 16
LOG2_E = 1.4426950408889634


def pieces(value, count):
    parts = []
    for k in range(count):
        part = value.astype(bf16)
        parts.append(part)
        if k < count - 1:
            value = value - part.astype(f32)
    return jnp.concatenate(parts, axis=1)


def columns_of(rows):
    return jnp.concatenate([rows, jnp.zeros((LANES - HEADS, T), f32)], axis=0).T


def set_heads(head_ref, head_t, until):
    turned = jnp.concatenate([head_ref[...], jnp.zeros((LANES - 8, LANES), f32)], axis=0).T
    head_t[0] = spread(turned[:, 0:1])[:HEADS]
    head_t[1] = spread(turned[:, 1:2])[:HEADS]
    matrix = jnp.where(block_iota(0) <= block_iota(1), 1.0, 0.0).astype(bf16)
    for k in range(3):
        until[k * T : (k + 1) * T, :] = matrix


def head_rows(dr_ref, head_t, until, rows):
    raw = dr_ref[rows, :].T[:HEADS] + head_t[0]
    dt = softplus(raw)
    decay = mm(pieces(dt * (head_t[1] * LOG2_E), 3), until[...])
    return raw, dt, decay, columns_of(dt), columns_of(decay)


def ring_place(n):
    me = lax.axis_index("dp")
    z, x = lax.div(me, 2), lax.rem(me, 2)
    return z + x * (n - 1 - 2 * z)


def ring_index(pos, n):
    back = lax.div(pos, n // 2)
    return 2 * pos + back * (2 * n - 1 - 4 * pos)


def neighbours(n):
    pos = ring_place(n)
    right = ring_index(lax.rem(pos + 1, n), n)
    left = ring_index(lax.rem(pos + n - 1, n), n)
    me = lax.axis_index("tensor")
    y, core = lax.div(me, 2), lax.rem(me, 2)
    across = 2 * (1 - y) + core
    beside = 2 * y + 1 - core
    return pos, ({"dp": right}, {"dp": left}), me, {"tensor": across}, {"tensor": beside}


def greet(peers):
    barrier = pltpu.get_barrier_semaphore()
    for peer in peers:
        pl.semaphore_signal(barrier, inc=1, device_id=peer, device_id_type=pl.DeviceIdType.MESH)


def enter(peers):
    greet(peers)
    pl.semaphore_wait(pltpu.get_barrier_semaphore(), len(peers))


def remote(src, dst, send_sem, recv_sem, peer):
    return pltpu.make_async_remote_copy(
        src_ref=src, dst_ref=dst, send_sem=send_sem, recv_sem=recv_sem,
        device_id=peer, device_id_type=pl.DeviceIdType.MESH,
    )


def span(start, size):
    return pl.ds(pl.multiple_of(start, 16), size)


def strip(rows):
    return next(size for size in (48, 32, 16) if rows % size == 0)


def cut_rows(rows):
    top = rows // 32 * 16
    return ((0, top), (top, rows - top))


def forward_body(
    n, rows, tokens, width,
    in_ref, cot_ref, flat_ref, wzx_ref, wbc_ref, wdt_ref, wout_ref,
    v_ref, xc_ref, dr_ref, st_ref, dy_ref, dz_ref, branch_ref, early_ref, gate_ref, gain_ref,
    xg_ref, ws_ref, wps_ref, taps_ref, head_ref, chan_ref,
    halo, state, y_all, z_all, dn_all, nl_all, dz_all, xg, cots, ws, wps, sums, red, head_t, until, across_state, tails,
    own_keep, early_keep, lead_keep, lead_send, lead_recv, x_keep, x_over_send, x_over_recv, x_side_send, x_side_recv,
    x_pass_send, x_pass_recv, ring_keep, ring_send, ring_recv, over_send, over_recv,
    side_send, side_recv, pass_send, pass_recv, sum_send, sum_recv,
):
    pairs = width // LANES
    wide = width + 2 * NS
    step = pl.program_id(0)
    steps = LEN // ROWS
    tall = 2 * ROWS
    norming = steps // 2
    gating = norming + 1
    forming = gating + 1
    products = forming + steps // 2
    pos, ring, me, across, beside = neighbours(n)
    opposite = lax.rem(me + 2, 4)
    next_door = me + 1 - 2 * lax.rem(me, 2)
    far = lax.rem(next_door + 2, 4)
    askew = {"tensor": far}
    quarter = tokens // 4
    hops = n // 2
    cuts = cut_rows(rows)
    mine = ring_index(pos, n)

    late = wide + LANES
    parts_of = ((0, width), (width, width))

    def hop(k, part, way, h):
        first, size = cuts[part]
        cols = pl.ds(*parts_of[k])
        block = ring_index(lax.rem(pos + (h if way else n - h), n), n)
        here = wps.at[span(block * rows + first, size), cols]
        return remote(here, here, ring_send.at[way, part, k, h], ring_recv.at[way, part, k, h], ring[way])

    def hop_lands(k, part, way, h):
        first, size = cuts[part]
        block = ring_index(lax.rem(pos + (h + 1 if way else n - h - 1), n), n)
        return span(block * rows + first, size), pl.ds(*parts_of[k])

    def hop_arrival(k, part, way, h):
        here = wps.at[hop_lands(k, part, way, h)]
        return remote(here, here, ring_send.at[way, part, k, h], ring_recv.at[way, part, k, h], ring[way])

    def hop_keep(part, way, h):
        at = hop_lands(1, part, way, h)
        return pltpu.make_async_copy(wps.at[at], wps_ref.at[at], ring_keep.at[way, part, h])

    def hop_ways(h):
        return [(part, way) for part in (0, 1) for way in (0, 1) if h < hops - 1 or part == way]

    def hop_on(k, h):
        for part, way in hop_ways(h - 1) if h > 0 else ():
            hop_arrival(k, part, way, h - 1).wait_recv()
            if k == 1:
                hop_keep(part, way, h - 1).start()
            if h < hops and (part, way) in hop_ways(h):
                hop(k, part, way, h).start()
        if h == 0:
            for part, way in hop_ways(0):
                hop(k, part, way, 0).start()

    def over(k):
        return remote(
            cot_ref.at[pl.ds(k * quarter, quarter)], cots.at[span(me * tokens + k * quarter, quarter)],
            over_send.at[k], over_recv.at[k], across,
        )

    def landed(start, size, send, recv, peer):
        here = cots.at[span(start, size)]
        return remote(here, here, send, recv, peer)

    def over_arrival(k):
        return landed(opposite * tokens + k * quarter, quarter, over_send.at[k], over_recv.at[k], across)

    def passing(k):
        return landed(opposite * tokens + k * quarter, quarter, pass_send.at[k], pass_recv.at[k], beside)

    def pass_arrival(k):
        return landed(far * tokens + k * quarter, quarter, pass_send.at[k], pass_recv.at[k], beside)

    def side():
        return remote(cot_ref, cots.at[span(me * tokens, tokens)], side_send.at[0], side_recv.at[0], beside)

    def side_arrival():
        return landed(next_door * tokens, tokens, side_send.at[0], side_recv.at[0], beside)

    def own_cot():
        return pltpu.make_async_copy(cot_ref, cots.at[span(me * tokens, tokens)], own_keep.at[0])

    def own_z():
        at = span(mine * rows, rows), pl.ds(*parts_of[1])
        return pltpu.make_async_copy(wps.at[at], wps_ref.at[at], own_keep.at[1])

    def pass_on(*pieces):
        for k in pieces:
            over_arrival(k).wait_recv()
            passing(k).start()

    def normalize(k):
        def some(i, _):
            at = span(me * tokens + k * quarter + i * 64, 64)
            squares = jnp.zeros((64, LANES), f32)
            for c in range(D // LANES):
                x = xg[at, c * LANES : (c + 1) * LANES].astype(f32)
                squares = squares + x * x
            inverse = lax.rsqrt(jnp.sum(squares, axis=-1, keepdims=True) / D + norm_eps)
            inverse = jnp.broadcast_to(inverse, (64, LANES))
            for c in range(D // LANES):
                cols = slice(c * LANES, (c + 1) * LANES)
                xg[at, cols] = (xg[at, cols].astype(f32) * inverse * flat_ref[c : c + 1, :]).astype(bf16)
            return 0

        lax.fori_loop(0, quarter // 64, some, 0)

    @pl.when(step == 0)
    def _():
        own_rows = span(me * tokens, tokens)
        greet((*ring, across, beside, askew))
        load = pltpu.make_async_copy(in_ref, xg.at[own_rows], own_keep.at[2])
        load.start()
        own_cot().start()
        mine_at = span(mine * rows, rows)
        ws[mine_at, :width] = wzx_ref[:, 1, :].astype(bf16)
        ws[mine_at, width:wide] = wbc_ref[...].astype(bf16)
        heads = wdt_ref.shape[0]
        unit = jnp.where(
            lax.broadcasted_iota(jnp.int32, (16, LANES), 0) == lax.broadcasted_iota(jnp.int32, (16, LANES), 1), 1.0, 0.0
        ).astype(bf16)
        steps_w = jnp.concatenate([wdt_ref[...], jnp.zeros((16 - heads, rows), f32)], axis=0).astype(bf16)
        ws[mine_at, wide:] = mm(steps_w, unit, TN).astype(bf16)
        load.wait()
        normalize(0)
        pl.semaphore_wait(pltpu.get_barrier_semaphore(), 5)
        started, kept = [], []

        def go(*args):
            copy = remote(*args)
            copy.start()
            started.append(copy)

        def keep(src, dst, sem):
            copy = pltpu.make_async_copy(src, dst, sem)
            copy.start()
            kept.append(copy)

        def arrived(part, way, h, block):
            first, size = cuts[part]
            at = span(block * rows + first, size)
            remote(
                ws.at[at], ws.at[at], lead_send.at[way, part, h], lead_recv.at[way, part, h], ring[way]
            ).wait_recv()
            keep(ws.at[at], ws_ref.at[at], lead_keep.at[way, part, h])

        def lead(h, parts=(0, 1)):
            for part in parts:
                first, size = cuts[part]
                for way in (0, 1):
                    block = ring_index(lax.rem(pos + (h if way else n - h), n), n)
                    here = ws.at[span(block * rows + first, size)]
                    if h > 0:
                        arrived(part, way, h - 1, block)
                    if h == hops - 1 and part != way:
                        continue
                    go(here, here, lead_send.at[way, part, h], lead_recv.at[way, part, h], ring[way])

        def x_over(k):
            at = span(me * tokens + k * quarter, quarter)
            go(xg.at[at], xg.at[at], x_over_send.at[k], x_over_recv.at[k], across)

        def x_pass(k):
            at = span(opposite * tokens + k * quarter, quarter)
            here = xg.at[at]
            remote(here, here, x_over_send.at[k], x_over_recv.at[k], across).wait_recv()
            go(here, here, x_pass_send.at[k], x_pass_recv.at[k], beside)
            keep(here, xg_ref.at[at], x_keep.at[k])

        def x_pass_lands(k):
            at = span(far * tokens + k * quarter, quarter)
            remote(xg.at[at], xg.at[at], x_pass_send.at[k], x_pass_recv.at[k], beside).wait_recv()
            keep(xg.at[at], xg_ref.at[at], x_keep.at[4 + k])

        lead(0, (0,))
        leading = list(started)
        x_over(0)
        for k in (1, 2, 3):
            normalize(k)
            if k == 1:
                x_over(1)
        go(xg.at[own_rows], xg.at[own_rows], x_side_send.at[0], x_side_recv.at[0], beside)
        keep(xg.at[own_rows], xg_ref.at[own_rows], x_keep.at[8])
        wps[mine_at, :width] = wout_ref[...].astype(bf16)
        wps[mine_at, width:] = wzx_ref[:, 0, :].astype(bf16)
        for copy in leading:
            copy.wait_send()
            started.remove(copy)
        lead(0, (1,))
        keep(ws.at[mine_at], ws_ref.at[mine_at], x_keep.at[9])
        own_z().start()
        halo[0:8, :] = jnp.zeros((8, wide), f32)
        state[...] = jnp.zeros_like(state)
        gate_ref[...] = jnp.zeros_like(gate_ref)
        parameter_rows(me, width, flat_ref, taps_ref, head_ref, chan_ref)
        set_heads(head_ref, head_t, until)
        lead(1)
        x_over(2)
        at = span(next_door * tokens, tokens)
        remote(xg.at[at], xg.at[at], x_side_send.at[0], x_side_recv.at[0], beside).wait_recv()
        keep(xg.at[at], xg_ref.at[at], x_keep.at[10])
        side().start()
        lead(2)
        x_over(3)
        x_pass(0)
        x_pass(1)
        for h in range(3, hops):
            lead(h)
        hop_on(0, 0)
        x_pass(2)
        over(0).start()
        x_pass_lands(0)
        x_pass_lands(1)
        x_pass(3)
        for part in (0, 1):
            arrived(part, part, hops - 1, ring_index(lax.rem(pos + n // 2, n), n))
        hop_on(1, 0)
        over(1).start()
        x_pass_lands(2)
        x_pass_lands(3)
        for copy in kept:
            copy.wait()
        for copy in started:
            copy.wait_send()

    def at_tick(tick):
        for k, times in enumerate(((1, 5), (3, 6))):
            for h in (1, 2):
                pl.when(tick == times[h - 1])(functools.partial(hop_on, k, h))

        @pl.when(tick == 2)
        def _():
            over(2).start()

        @pl.when(tick == 4)
        def _():
            over(3).start()
            pass_on(0, 1)

        pl.when(tick == steps - 1)(functools.partial(pass_on, 2))

    @pl.when(step < norming)
    def _():
        def chunk(i, _):
            tick = 2 * step + i
            at_tick(tick)
            scan_step(
                width, tick, i, xg, ws, taps_ref, head_ref, chan_ref,
                v_ref, xc_ref, dr_ref, st_ref, halo, state, y_all, head_t, until, across_state, tails,
                functools.partial(pass_on, 3),
            )
            return 0

        lax.fori_loop(0, 2, chunk, 0)

    @pl.when(step == norming)
    def _():
        for h in range(3, hops):
            for k in (0, 1):
                hop_on(k, h)
        hop_on(0, hops)
        side_arrival().wait_recv()
        for k in range(4):
            pass_arrival(k).wait_recv()
        own_cot().wait()
        own_z().wait()

        def some(i, _):
            at = span(i * tall, tall)
            dn_all[at, :] = mm(cots[at, :], wps[:, :width]).astype(bf16)
            return 0

        lax.fori_loop(0, LEN // tall, some, 0)

    @pl.when(step == gating)
    def _():
        hop_on(1, hops)
        ones = jnp.ones((8, LANES), f32)

        def some(i, _):
            at = span(i * tall, tall)
            z_all[at, :] = mm(xg[at, :], wps[:, width:])
            for sub in range(tall // T):
                rows_at = span(i * tall + sub * T, T)
                squares = jnp.zeros((T, LANES), f32)
                inner = jnp.zeros((T, LANES), f32)
                for p in range(pairs):
                    cols = slice(p * LANES, (p + 1) * LANES)
                    z = z_all[rows_at, cols]
                    gated = y_all[rows_at, cols] * (z * sigmoid(z))
                    squares = squares + gated * gated
                    inner = inner + gated * chan_ref[0:1, cols] * dn_all[rows_at, cols].astype(f32)
                lanes = pl.ds(pl.multiple_of(i * tall + sub * T, T), T)
                sums[me, 0:4, lanes] = mm_exact(ones, squares, NT)[0:4]
                sums[me, 4:8, lanes] = mm_exact(ones, inner, NT)[4:8]
            return 0

        lax.fori_loop(0, LEN // tall, some, 0)

    @pl.when(step == forming - 1)
    def _():
        peers = ((beside, next_door), (across, opposite), (askew, far))
        for k, (peer, _) in enumerate(peers):
            remote(sums.at[me], sums.at[me], sum_send.at[k], sum_recv.at[k], peer).start()
        for h in range(hops):
            for part, way in hop_ways(h):
                for k in (0, 1):
                    hop(k, part, way, h).wait_send()
                hop_keep(part, way, h).wait()
        side().wait_send()
        for k in range(4):
            over(k).wait_send()
            passing(k).wait_send()
        for k, (peer, other) in enumerate(peers):
            remote(sums.at[other], sums.at[other], sum_send.at[k], sum_recv.at[k], peer).wait()
        red[...] = ((sums[0] + sums[1]) + sums[2]) + sums[3]

    @pl.when((step >= forming) & (step < products))
    def _():
        def some(i, _):
            first = (step - forming) * tall + i * ROWS
            lanes = pl.ds(pl.multiple_of(first, ROWS), ROWS)
            q_row = lax.rsqrt(red[0:4, lanes] / DI + norm_eps)
            k_row = q_row * q_row * q_row * red[4:8, lanes] / DI
            turned = jnp.concatenate([q_row, k_row], axis=0).T
            for sub in range(ROWS // T):
                rows_at = slice(sub * T, (sub + 1) * T)
                at = span(first + sub * T, T)
                q, kk = spread(turned[rows_at, 0:1]), spread(turned[rows_at, 4:5])
                for p in range(pairs):
                    cols = slice(p * LANES, (p + 1) * LANES)
                    z, y, dn = z_all[at, cols], y_all[at, cols], dn_all[at, cols].astype(f32)
                    gain = chan_ref[0:1, cols]
                    s = sigmoid(z)
                    sz = z * s
                    gated = y * sz
                    gq = gated * q
                    dg = q * gain * dn - gated * kk
                    gate_ref[:, cols] += jnp.sum((gq * dn).reshape(T // 8, 8, LANES), axis=0)
                    nl_all[at, cols] = (gq * gain).astype(bf16)
                    dz_all[at, cols] = (dg * y * (s + sz * (1.0 - s))).astype(bf16)
                    dn_all[at, cols] = (dg * sz).astype(bf16)
            branch_ref[span(i * ROWS, ROWS), :] = mm(nl_all[span(first, ROWS), :], wps[:, :width], NT).astype(bf16)
            return 0

        lax.fori_loop(0, 2, some, 0, unroll=2)

    def rows_out():
        return [
            pltpu.make_async_copy(src, dst, own_keep.at[2 + k])
            for k, (src, dst) in enumerate(((dz_all, dz_ref), (dn_all, dy_ref)))
        ]

    def early_out(i):
        at = span(i * ROWS, ROWS)
        return [
            pltpu.make_async_copy(src.at[at, pl.ds(0, width)], early_ref.at[at, pl.ds(k * width, width)], early_keep.at[k, i])
            for k, src in enumerate((ws, wps))
        ]

    @pl.when(step == products)
    def _():
        for copy in rows_out():
            copy.start()

        def some(i, _):
            at = span(i * ROWS, ROWS)
            lanes = pl.ds(pl.multiple_of(i * ROWS, ROWS), ROWS)
            grad = mm(xg[:, lanes], dz_all[...], TN)
            ws[at, :width] = grad.astype(bf16)
            share = jnp.zeros((ROWS, LANES), f32)
            for p in range(pairs):
                cols = slice(p * LANES, (p + 1) * LANES)
                w = wps[at, width + p * LANES : width + (p + 1) * LANES]
                share = share + grad[:, cols] * w.astype(f32)
            gain_ref[:, lanes] = mm_exact(jnp.ones((8, LANES), f32), share, NT)
            wps[at, :width] = mm(cots[:, lanes], nl_all[...], TN).astype(bf16)
            for copy in early_out(i):
                copy.start()
            return 0

        lax.fori_loop(0, D // ROWS, some, 0, unroll=3)
        for copy in rows_out():
            copy.wait()

        def done(i, _):
            for copy in early_out(i):
                copy.wait()
            return 0

        lax.fori_loop(0, D // ROWS, done, 0)


def parameter_rows(me, width, flat_ref, taps_ref, head_ref, chan_ref):
    pairs = width // LANES
    heads = width // P_SIZE
    taps_ref[...] = jnp.zeros_like(taps_ref)
    chan_ref[...] = jnp.zeros_like(chan_ref)
    for c in range(pairs):
        cols = slice(c * LANES, (c + 1) * LANES)
        chan_ref[0:1, cols] = flat_ref[pl.ds(GATE_ROW + pairs * me + c, 1), :]
        taps_ref[CONV : CONV + 1, cols] = flat_ref[pl.ds(BIAS_ROW + pairs * me + c, 1), :]
        for k in range(CONV):
            taps_ref[k : k + 1, cols] = flat_ref[pl.ds(TAPS_ROW + 4 * pairs * k + pairs * me + c, 1), :]
    for c in range(2):
        cols = slice(width + c * LANES, width + (c + 1) * LANES)
        taps_ref[CONV : CONV + 1, cols] = flat_ref[BIAS_BC_ROW + c : BIAS_BC_ROW + c + 1, :]
        for k in range(CONV):
            row = TAPS_BC_ROW + 2 * k + c
            taps_ref[k : k + 1, cols] = flat_ref[row : row + 1, :]
    both = jnp.concatenate([flat_ref[HEAD_ROW : HEAD_ROW + 1, :], flat_ref[HEAD_ROW + 1 : HEAD_ROW + 2, :]], axis=1)
    both = jnp.broadcast_to(both, (8, 2 * LANES))
    lane = lax.broadcasted_iota(jnp.int32, (2 * LANES, LANES), 0)
    head = lax.broadcasted_iota(jnp.int32, (2 * LANES, LANES), 1)

    def take(kind):
        match = (lane == 4 * heads * kind + heads * me + head) & (head < heads)
        return mm_exact(both, jnp.where(match, 1.0, 0.0).astype(f32))

    valid = lax.broadcasted_iota(jnp.int32, (8, LANES), 1) < heads
    row = lax.broadcasted_iota(jnp.int32, (8, LANES), 0)
    rates = jnp.where(valid, -jnp.exp(take(1)), 0.0)
    head_ref[...] = jnp.where(row == 0, take(0), jnp.where(row == 1, rates, 0.0))
    skip = mm_exact(take(2), picked(width).astype(f32), NT)
    chan_ref[1:2, :] = skip[0:1]


def picked(width):
    channel = lax.broadcasted_iota(jnp.int32, (width, LANES), 0)
    head = lax.broadcasted_iota(jnp.int32, (width, LANES), 1)
    return jnp.where((channel >= head * P_SIZE) & (channel < (head + 1) * P_SIZE), 1.0, 0.0).astype(bf16)


def scan_step(
    width, tick, i, xg, w_ref, taps_ref, head_ref, chan_ref,
    v_ref, xc_ref, dr_ref, st_ref, halo, state, y_all, head_t, until, across_state, tails, late_turn,
):
    pairs = width // LANES
    wide = width + 2 * NS
    mine = span(tick * ROWS, ROWS)
    dr_ref[span(i * ROWS, ROWS), :] = mm(xg[mine, :], w_ref[:, wide:])
    halo[8 : 8 + ROWS, :] = mm(xg[mine, :], w_ref[:, :wide])
    low_half = block_iota(1) < P_SIZE
    causal = block_iota(0) >= block_iota(1)

    def convolved(sub, block):
        cols = slice(block * LANES, (block + 1) * LANES)
        total = taps_ref[CONV : CONV + 1, cols]
        for k in range(CONV):
            first = 8 - (CONV - 1) + k + sub * T
            total = total + taps_ref[k : k + 1, cols] * halo[first : first + T, cols]
        rows = span(i * ROWS + sub * T, T)
        xc_ref[rows, cols] = total.astype(bf16)
        v_ref[rows, cols] = halo[8 + sub * T : 8 + (sub + 1) * T, cols].astype(bf16)
        return total * sigmoid(total)

    for sub in range(ROWS // T):
        rows = span(i * ROWS + sub * T, T)
        _, _, decay_t, dt, decay = head_rows(dr_ref, head_t, until, rows)
        b_low = convolved(sub, pairs).astype(bf16)
        c_low = convolved(sub, pairs + 1).astype(bf16)
        b_t = b_low.T
        scores = jnp.where(causal, mm(c_low, b_low, NT), 0.0)
        entering = state[...].astype(bf16)
        st_ref[i * (ROWS // T) + sub] = entering
        across_state[...] = mm(c_low, entering)
        for p in range(pairs):
            cols = slice(p * LANES, (p + 1) * LANES)
            x = convolved(sub, p)
            l1, l2 = spread(decay[:, 2 * p : 2 * p + 1]), spread(decay[:, 2 * p + 1 : 2 * p + 2])
            both = jnp.where(low_half, l1, l2)
            dtb = jnp.where(
                low_half, spread(dt[:, 2 * p : 2 * p + 1]), spread(dt[:, 2 * p + 1 : 2 * p + 2])
            )
            u = x * dtb
            m1 = scores * jnp.exp2(jnp.minimum(l1 - decay_t[2 * p : 2 * p + 1, :], 0.0))
            m2 = scores * jnp.exp2(jnp.minimum(l2 - decay_t[2 * p + 1 : 2 * p + 2, :], 0.0))
            mixing = jnp.concatenate([m1.astype(bf16), m2.astype(bf16)], axis=1)
            u_low = u.astype(bf16)
            zero = jnp.zeros_like(u_low)
            parts = jnp.concatenate(
                [jnp.where(low_half, u_low, zero), jnp.where(low_half, zero, u_low)], axis=0
            )
            last = both[T - 1 : T, :]
            y = mm(mixing, parts) + jnp.exp2(both) * across_state[:, cols] + chan_ref[1:2, cols] * x
            tails[:, cols] = (u * jnp.exp2(last - both)).astype(bf16)
            state[:, cols] = jnp.exp2(last) * state[:, cols]
            y_all[span(tick * ROWS + sub * T, T), cols] = y
        state[...] = state[...] + mm(b_t, tails[...])
        if sub == 0:
            pl.when(tick == LEN // ROWS - 1)(late_turn)
    halo[0:8, :] = halo[ROWS : ROWS + 8, :]


def ssd_forward(n, layer_input, out_grad, flat, w_zx, w_bc, w_dt, w_out):
    rows, width = w_out.shape
    tokens = layer_input.shape[0]
    length = 4 * tokens
    wide = width + 2 * NS
    tall = 2 * ROWS
    steps = length // tall
    forming = steps + 2
    products = forming + steps
    subs = tall // T
    assert length == LEN
    row = lambda m: pl.BlockSpec((tall, m), lambda i: (jnp.minimum(i, steps - 1), 0))
    form = lambda m: pl.BlockSpec((tall, m), lambda i: (jnp.clip(i - forming, 0, steps - 1), 0))
    whole = lambda a: pl.BlockSpec(a.shape, lambda i: (0,) * a.ndim, pipeline_mode=pl.Buffered(1))
    fixed = lambda m: pl.BlockSpec((8, m), lambda i: (0, 0))
    anywhere = pl.BlockSpec(memory_space=pl.ANY)
    vm, dma = pltpu.VMEM, pltpu.SemaphoreType.DMA
    hops, lead = dma((2, 2, 2, n // 2)), dma((2, 2, n // 2))
    shape = lambda dims, dtype: jax.ShapeDtypeStruct(dims, dtype)
    return pl.pallas_call(
        functools.partial(forward_body, n, rows, tokens, width),
        grid=(products + 1,),
        in_specs=[anywhere, anywhere, *(whole(a) for a in (flat, w_zx, w_bc, w_dt, w_out))],
        out_specs=[
            row(wide), row(wide), row(LANES), pl.BlockSpec((subs, NS, width), lambda i: (jnp.minimum(i, steps - 1), 0, 0)),
            anywhere, anywhere, form(D), anywhere,
            fixed(width), fixed(D), anywhere, anywhere, anywhere, *(fixed(m) for m in (wide, LANES, width)),
        ],
        out_shape=[
            shape((length, wide), bf16), shape((length, wide), bf16), shape((length, LANES), f32),
            shape((length // T, NS, width), bf16), shape((length, width), bf16), shape((length, width), bf16),
            shape((length, D), bf16), shape((D, 2 * width), bf16), shape((8, width), f32), shape((8, D), f32),
            shape((length, D), bf16), shape((D, wide + LANES), bf16), shape((D, 2 * width), bf16),
            *(shape((8, m), f32) for m in (wide, LANES, width)),
        ],
        scratch_shapes=[
            vm((ROWS + 8, wide), f32), vm((NS, width), f32), vm((length, width), f32), vm((length, width), f32),
            *(vm((length, width), bf16) for _ in range(3)),
            vm((length, D), bf16), vm((length, D), bf16), vm((D, wide + LANES), bf16), vm((D, 2 * width), bf16),
            vm((4, 8, length), f32), vm((8, length), f32), vm((2, HEADS, LANES), f32), vm((3 * T, LANES), bf16),
            vm((T, width), f32), vm((T, width), bf16),
            dma((4,)), dma((2, D // ROWS)), lead, lead, lead, dma((11,)), dma((4,)), dma((4,)), dma((1,)), dma((1,)),
            dma((4,)), dma((4,)), lead, hops, hops, dma((4,)), dma((4,)),
            dma((1,)), dma((1,)), dma((4,)), dma((4,)), dma((3,)), dma((3,)),
        ],
        compiler_params=pltpu.CompilerParams(collective_id=2, has_side_effects=True, vmem_limit_bytes=ROOM),
        name="layer_forward",
    )(layer_input, out_grad, flat, w_zx, w_bc, w_dt, w_out)


def backward_body(
    n, own_rows, tokens, width,
    dy_ref, v_ref, xc_ref, dr_ref, st_ref, gate_ref, taps_ref, head_ref, chan_ref, early_ref, branch_ref,
    d_ref, small_ref, oearly_ref, obranch_ref,
    dxh, dstate, yst, bds, dyeb, utb, products, turn, acc, hacc, pick_ref, pick_t, fades, head_t, until_ref, reach_ref,
    own, slots, near, held, over_slot,
    load_sem, ring_send, ring_recv, near_send, near_recv, over_send, over_recv,
):
    pairs = width // LANES
    wide = width + 2 * NS
    step = pl.program_id(0)
    steps = LEN // ROWS
    subs = ROWS // T
    pos, ring, me, across, beside = neighbours(n)
    opposite = lax.rem(me + 2, 4)
    next_door = me + 1 - 2 * lax.rem(me, 2)
    far = lax.rem(next_door + 2, 4)
    half = tokens // 2
    cuts = cut_rows(own_rows)

    def block_at(way, count):
        return ring_index(lax.rem(pos + (count if way else n - count), n), n)

    def hop(k, way, h):
        first, size = cuts[way]
        if h == 0:
            src = early_ref.at[span(block_at(way, 1) * own_rows + first, size), pl.ds(k * width, width)]
        else:
            src = slots[way][k].at[h - 1]
        return remote(
            src, slots[way][k].at[h], ring_send.at[way, k, h], ring_recv.at[way, k, h], ring[way]
        )

    def near_copy(turned, part):
        start = (next_door if turned else far) * tokens + part * half
        return remote(
            branch_ref.at[span(start, half)], near.at[turned, part],
            near_send.at[turned, part], near_recv.at[turned, part], beside,
        )

    def held_copy(turned, part):
        start = (me if turned else opposite) * tokens + part * half
        return pltpu.make_async_copy(
            branch_ref.at[span(start, half)], held.at[turned, part], load_sem.at[2 * turned + part]
        )

    def over_copy(part):
        return remote(held.at[0, part], over_slot.at[part], over_send.at[part], over_recv.at[part], across)

    def own_copy():
        return pltpu.make_async_copy(early_ref, own, load_sem.at[4])

    def ring_turn(k, h):
        for way in (0, 1):
            first, size = cuts[way]
            hop(k, way, h).wait_recv()
            block = block_at(way, 2 + h) if h < n - 2 else block_at(way, 0)

            tile = strip(size)

            def some(i, _, way=way, first=first, block=block, tile=tile):
                cols = slice(k * width, (k + 1) * width)
                came = slots[way][k][h, span(i * tile, tile), :]
                mine = own[span(block * own_rows + first + i * tile, tile), cols]
                if h < n - 2:
                    slots[way][k][h, span(i * tile, tile), :] = came + mine
                else:
                    oearly_ref[span(first + i * tile, tile), cols] = came.astype(f32) + mine.astype(f32)
                return 0

            lax.fori_loop(0, size // tile, some, 0)
            if h < n - 2:
                hop(k, way, h + 1).start()

    def ring_poll(k, tick):
        for h in range(n - 1):
            pl.when(tick == min(h + 1, steps - 1))(functools.partial(ring_turn, k, h))

    def add_near(turned):
        for part in (0, 1):
            held_copy(turned, part).wait()
            near_copy(turned, part).wait_recv()

            def some(i, _, part=part):
                at = span(i * 32, 32)
                held[turned, part, at, :] = held[turned, part, at, :] + near[turned, part, at, :]
                return 0

            lax.fori_loop(0, half // 32, some, 0)
            if not turned:
                over_copy(part).start()

    @pl.when(step == 0)
    def _():
        enter((*ring, across, beside))
        for way in (0, 1):
            hop(0, way, 0).start()
        for turned in (0, 1):
            for part in (0, 1):
                near_copy(turned, part).start()
                held_copy(turned, part).start()
        own_copy().start()
        dxh[T : T + 8, :] = jnp.zeros((8, wide), f32)
        dstate[...] = jnp.zeros_like(dstate)
        acc[...] = jnp.zeros_like(acc)
        hacc[...] = jnp.zeros_like(hacc)
        turn[...] = jnp.zeros_like(turn)
        pick_ref[...] = picked(width)
        channel = lax.broadcasted_iota(jnp.int32, (HEADS, width), 1)
        head = lax.broadcasted_iota(jnp.int32, (HEADS, width), 0)
        mine = (channel >= head * P_SIZE) & (channel < (head + 1) * P_SIZE)
        pick_t[...] = jnp.where(mine, 1.0, 0.0).astype(bf16)
        set_heads(head_ref, head_t, until_ref)
        from_here = jnp.where(block_iota(0) >= block_iota(1), 1.0, 0.0).astype(bf16)
        after = jnp.where(block_iota(0) < block_iota(1), 1.0, 0.0).astype(bf16)
        for k, matrix in enumerate((from_here, from_here, after, after)):
            reach_ref[k * T : (k + 1) * T, :] = matrix
        products[3 * T :, :] = jnp.zeros((HEADS, width), bf16)

    low_half = block_iota(1) < P_SIZE
    row_at, col_at = block_iota(0), block_iota(1)
    until = row_at <= col_at
    pair_lane = lax.broadcasted_iota(jnp.int32, (8, 2 * T), 1)
    pair_row = lax.broadcasted_iota(jnp.int32, (8, 2 * T), 0)
    each = jnp.where(lax.div(pair_lane, T) == pair_row, 1.0, 0.0).astype(bf16)
    ones = jnp.ones((8, T), bf16)

    def add(index, cols, value):
        acc[index, :, cols] += jnp.sum(value.reshape(T // 8, 8, LANES), axis=0)

    def conv_back(rows, block, d_act, xc, s, act):
        cols = slice(block * LANES, (block + 1) * LANES)
        dxh[0:T, cols] = d_act * (s + act * (1.0 - s))
        v = v_ref[rows, cols].astype(f32)
        total = None
        for m in range(CONV):
            moved = dxh[m : m + T, cols]
            if m == 0:
                add(CONV, cols, moved)
            add(CONV - 1 - m, cols, v * moved)
            term = taps_ref[CONV - 1 - m : CONV - m, cols] * moved
            total = term if total is None else total + term
        d_ref[rows, cols] = total.astype(bf16)

    def work(i, _):
        tick = 2 * step + i
        chunk = 1 - i

        @pl.when(tick == 1)
        def _():
            own_copy().wait()
            add_near(0)

        pl.when(tick == 2)(functools.partial(add_near, 1))
        ring_poll(0, tick)
        for sub in reversed(range(subs)):
            rows = span(chunk * ROWS + sub * T, T)
            block_state = chunk * subs + sub
            raw_t, dt_t, decay_t, dt, decay = head_rows(dr_ref, head_t, until_ref, rows)
            b_cols = slice(width, width + NS)
            c_cols = slice(width + NS, width + 2 * NS)
            b_xc, c_xc = xc_ref[rows, b_cols].astype(f32), xc_ref[rows, c_cols].astype(f32)
            b_s, c_s = sigmoid(b_xc), sigmoid(c_xc)
            b_act, c_act = b_xc * b_s, c_xc * c_s
            b_low, c_low = b_act.astype(bf16), c_act.astype(bf16)
            c_t = c_low.T
            scores_t = jnp.where(until, mm(b_low, c_low, NT), 0.0)
            ds_low = dstate[...].astype(bf16)
            yst[...] = mm(c_low, st_ref[block_state])
            bds[...] = mm(b_low, ds_low)
            d_scores = jnp.zeros((T, LANES), f32)
            for p in range(pairs):
                cols = slice(p * LANES, (p + 1) * LANES)
                dy_low = dy_ref[rows, cols]
                dy = dy_low.astype(f32)
                xc = xc_ref[rows, cols].astype(f32)
                xs = sigmoid(xc)
                x = xc * xs
                l1, l2 = spread(decay[:, 2 * p : 2 * p + 1]), spread(decay[:, 2 * p + 1 : 2 * p + 2])
                both = jnp.where(low_half, l1, l2)
                dtb = jnp.where(
                    low_half, spread(dt[:, 2 * p : 2 * p + 1]), spread(dt[:, 2 * p + 1 : 2 * p + 2])
                )
                u = x * dtb
                last = both[T - 1 : T, :]
                e1 = jnp.exp2(jnp.minimum(decay_t[2 * p : 2 * p + 1, :] - l1, 0.0))
                e2 = jnp.exp2(jnp.minimum(decay_t[2 * p + 1 : 2 * p + 2, :] - l2, 0.0))
                zero = jnp.zeros_like(dy_low)
                dy_parts = jnp.concatenate(
                    [jnp.where(low_half, dy_low, zero), jnp.where(low_half, zero, dy_low)], axis=0
                )
                du_in = mm(
                    jnp.concatenate([(scores_t * e1).astype(bf16), (scores_t * e2).astype(bf16)], axis=1), dy_parts
                )
                d_mix = mm(u.astype(bf16), dy_parts, NT)
                d1, d2 = d_mix[:, :T] * e1, d_mix[:, T:] * e2
                d_scores = d_scores + d1 + d2
                held_pairs = jnp.concatenate([(d1 * scores_t).astype(bf16), (d2 * scores_t).astype(bf16)], axis=1)
                reached_by = mm(ones, held_pairs)
                leaving = mm(each, held_pairs, NT)
                turn[2 * p : 2 * p + 1, :] = reached_by[0:1, :T] - leaving[0:1]
                turn[2 * p + 1 : 2 * p + 2, :] = reached_by[0:1, T:] - leaving[1:2]
                tail = jnp.exp2(last - both)
                fades[0:1, cols] = jnp.exp2(last)
                dye = dy * jnp.exp2(both)
                du_out = tail * bds[:, cols]
                du = du_in + du_out
                products[0:T, cols] = (dye * yst[:, cols]).astype(bf16)
                products[T : 2 * T, cols] = (u * du_out).astype(bf16)
                products[2 * T : 3 * T, cols] = (x * du).astype(bf16)
                dyeb[:, cols] = dye.astype(bf16)
                utb[:, cols] = (u * tail).astype(bf16)
                add(CONV + 1, cols, dy * x)
                conv_back(rows, p, dtb * du + chan_ref[1:2, cols] * dy, xc, xs, x)
            d_scores = jnp.where(until, d_scores, 0.0).astype(bf16)
            d_b = mm(d_scores, c_low) + mm(utb[...], ds_low, NT)
            d_c = mm(d_scores, b_low, TN) + mm(dyeb[...], st_ref[block_state], NT)
            conv_back(rows, pairs, d_b, b_xc, b_s, b_act)
            conv_back(rows, pairs + 1, d_c, c_xc, c_s, c_act)
            fade = fades[0:1, :]
            before_ds = dstate[...]
            through = jnp.sum(before_ds * st_ref[block_state].astype(f32), axis=0, keepdims=True) * fade
            products[3 * T : 3 * T + HEADS, :] = jnp.broadcast_to(through, (HEADS, width)).astype(bf16)
            dstate[...] = fade * before_ds + mm(c_t, dyeb[...])
            by_head = mm(pick_t[...], products[...], NT)
            inside = pieces(turn[...] + by_head[:, :T], 2)
            outside = pieces(by_head[:, T : 2 * T], 2)
            reached = mm(jnp.concatenate([inside, outside], axis=1), reach_ref[...])
            reached = reached + jnp.broadcast_to(by_head[:, 3 * T : 3 * T + 1], (HEADS, T))
            d_raw = (head_t[1] * reached + by_head[:, 2 * T : 3 * T]) * sigmoid(raw_t)
            d_ref[rows, wide:] = columns_of(d_raw).astype(bf16)
            hacc[0] += d_raw
            hacc[1] += dt_t * reached
            dxh[T : T + 8, :] = dxh[0:8, :]
            if sub == 1:
                @pl.when(tick == 0)
                def _():
                    for way in (0, 1):
                        hop(1, way, 0).start()

                ring_poll(1, tick)
        return 0

    lax.fori_loop(0, 2, work, 0)

    @pl.when(step == steps // 2 - 1)
    def _():
        total = lambda a: jnp.sum(a, axis=0, keepdims=True)
        for k in range(CONV + 1):
            small_ref[k : k + 1, :] = total(acc[k])
        small_ref[CONV + 1 : CONV + 2, :width] = total(gate_ref[...])
        small_ref[CONV + 1 : CONV + 2, width : width + LANES] = total(columns_of(hacc[0]))
        small_ref[CONV + 1 : CONV + 2, width + LANES :] = total(columns_of(hacc[1])) * head_ref[1:2, :]
        small_ref[CONV + 2 :, :] = jnp.zeros((2, wide), f32)
        skip = mm_exact(acc[CONV + 1, :, :width], pick_ref[...].astype(f32))
        small_ref[CONV + 3 : CONV + 4, 512 : 512 + LANES] = total(skip)
        for part in (0, 1):
            over_copy(part).wait_recv()

            def some(i, _, part=part):
                at = span(part * half + i * 32, 32)
                here = span(i * 32, 32)
                total = held[1, part, here, :].astype(f32) + over_slot[part, here, :].astype(f32)
                obranch_ref[at, :] = total.astype(bf16)
                return 0

            lax.fori_loop(0, half // 32, some, 0)
        for part in (0, 1):
            over_copy(part).wait_send()
            for turned in (0, 1):
                near_copy(turned, part).wait_send()
        for h in range(n - 1):
            for k in (0, 1):
                for way in (0, 1):
                    hop(k, way, h).wait_send()


def ssd_backward(n, dy, v, xc, dr, st, gate, taps, head, chan, early, branch):
    length, width = dy.shape
    wide = width + 2 * NS
    tall = 2 * ROWS
    steps = length // tall
    subs = tall // T
    own_rows, tokens = D // n, length // 4
    half = tokens // 2
    row = lambda m: pl.BlockSpec((tall, m), lambda i: (steps - 1 - i, 0))
    whole = lambda a: pl.BlockSpec(a.shape, lambda i: (0,) * a.ndim, pipeline_mode=pl.Buffered(1))
    fixed = lambda *shape: pl.BlockSpec(shape, lambda i: (0,) * len(shape))
    anywhere = pl.BlockSpec(memory_space=pl.ANY)
    vm, dma = pltpu.VMEM, pltpu.SemaphoreType.DMA
    return pl.pallas_call(
        functools.partial(backward_body, n, own_rows, tokens, width),
        grid=(steps,),
        in_specs=[
            row(width), row(wide), row(wide), row(LANES),
            pl.BlockSpec((subs, NS, width), lambda i: (steps - 1 - i, 0, 0)),
            whole(gate), whole(taps), whole(head), whole(chan), anywhere, anywhere,
        ],
        out_specs=[
            row(wide + LANES), fixed(8, wide), fixed(own_rows, 2 * width), fixed(tokens, D),
        ],
        out_shape=[
            jax.ShapeDtypeStruct((length, wide + LANES), bf16),
            jax.ShapeDtypeStruct((8, wide), f32),
            jax.ShapeDtypeStruct((own_rows, 2 * width), f32),
            jax.ShapeDtypeStruct((tokens, D), bf16),
        ],
        scratch_shapes=[
            vm((T + 8, wide), f32), vm((NS, width), f32), vm((T, width), f32), vm((T, width), f32),
            vm((T, width), bf16), vm((T, width), bf16), vm((3 * T + HEADS, width), bf16),
            vm((HEADS, T), f32), vm((CONV + 2, 8, wide), f32), vm((2, HEADS, T), f32),
            vm((width, LANES), bf16), vm((HEADS, width), bf16), vm((8, width), f32), vm((2, HEADS, LANES), f32),
            vm((3 * T, LANES), bf16), vm((4 * T, LANES), bf16),
            vm((D, 2 * width), bf16),
            [[vm((n - 1, size, width), bf16) for _ in (0, 1)] for _, size in cut_rows(own_rows)],
            vm((2, 2, half, D), bf16), vm((2, 2, half, D), bf16), vm((2, half, D), bf16),
            dma((5,)), dma((2, 2, n - 1)), dma((2, 2, n - 1)), dma((2, 2)), dma((2, 2)), dma((2,)), dma((2,)),
        ],
        compiler_params=pltpu.CompilerParams(
            collective_id=3, has_side_effects=True, vmem_limit_bytes=ROOM
        ),
        name="layer_backward",
    )(dy, v, xc, dr, st, gate, taps, head, chan, early, branch)


def reduce_body(
    n, rows, tokens, starts,
    xg_ref, d_ref, dz_ref, wp_ref, w_ref, small_ref, flat_ref, gain_ref,
    oxs_ref, oback_ref, bc_ref, oflat_ref,
    xg, d, dz, wz, w, work, grads, slots, staged, near, over, smalls, tens, bc_slot,
    load_sem, ring_send, ring_recv, near_send, near_recv, over_send, over_recv,
    small_send, small_recv, ten_send, ten_recv, bc_send, bc_recv,
):
    pos, ring, me, across, beside = neighbours(n)
    cuts = cut_rows(rows)
    core = lax.rem(me, 2)
    opposite = lax.rem(me + 2, 4)
    next_door = me + 1 - 2 * core
    far = lax.rem(next_door + 2, 4)
    half = tokens // 2
    late = d.shape[1]
    width = dz.shape[1]
    tile = 2 * LANES
    tiles = D // tile
    columns = [pl.ds(lo, hi - lo) for lo, hi in starts]
    sources = [(d_ref.at[:, columns[0]], d.at[:, columns[0]])]
    sources += [(xg_ref.at[:, pl.ds(i * tile, tile)], xg.at[:, pl.ds(i * tile, tile)]) for i in range(tiles)]
    sources += [(d_ref.at[:, some], d.at[:, some]) for some in columns[1:]]
    sources += [
        (dz_ref, dz), (w_ref, w), (wp_ref.at[:, pl.ds(width, width)], wz), (small_ref, smalls.at[pos]),
    ]
    loads = [pltpu.make_async_copy(src, dst, load_sem.at[k]) for k, (src, dst) in enumerate(sources)]
    for load in loads:
        load.start()
    askew = {"tensor": far}
    enter((*ring, across, beside, askew))
    started = []

    def go(*args):
        copy = remote(*args)
        copy.start()
        started.append(copy)

    def block_at(way, count):
        return ring_index(lax.rem(pos + (count if way else n - count), n), n)

    def hop(k, way, h):
        lo, hi = starts[k]
        first, size = cuts[way]
        if h == 0:
            src = grads.at[span(block_at(way, 1) * rows + first, size), pl.ds(lo, hi - lo)]
        else:
            src = slots[way][k].at[h - 1]
        return remote(
            src, slots[way][k].at[h], ring_send.at[way, k, h], ring_recv.at[way, k, h], ring[way]
        )

    def product(k):
        lo, hi = starts[k]

        def some(i, _):
            at = pl.ds(pl.multiple_of(i * tile, tile), tile)
            if k == 0:
                pltpu.make_async_copy(xg_ref.at[:, at], xg.at[:, at], load_sem.at[1 + i]).wait()
            grads[at, lo:hi] = mm(xg[:, at], d[:, lo:hi], TN).astype(bf16)
            return 0

        if k < 2:
            loads[0 if k == 0 else tiles + k].wait()
        lax.fori_loop(0, tiles, some, 0)
        for way in (0, 1):
            hop(k, way, 0).start()

    def near_copy(turned, part):
        return remote(
            staged.at[turned, part], near.at[turned, part],
            near_send.at[turned, part], near_recv.at[turned, part], beside,
        )

    def over_copy(part):
        return remote(near.at[0, part], over.at[part], over_send.at[part], over_recv.at[part], across)

    def ring_turn(k, h):
        lo, hi = starts[k]
        for way in (0, 1):
            first, size = cuts[way]
            slot = slots[way][k].at[h]
            remote(slot, slot, ring_send.at[way, k, h], ring_recv.at[way, k, h], ring[way]).wait_recv()
            block = block_at(way, 2 + h) if h < n - 2 else block_at(way, 0)

            tile = strip(size)

            def some(i, _, way=way, first=first, block=block, tile=tile):
                came = slots[way][k][h, span(i * tile, tile), :]
                mine = grads[span(block * rows + first + i * tile, tile), lo:hi]
                if h < n - 2:
                    slots[way][k][h, span(i * tile, tile), :] = came + mine
                else:
                    oxs_ref[span(first + i * tile, tile), lo:hi] = came.astype(f32) + mine.astype(f32)
                return 0

            lax.fori_loop(0, size // tile, some, 0)
            if h < n - 2:
                hop(k, way, h + 1).start()

    def small_hop(way, h):
        here = smalls.at[lax.rem(pos + (h if way else n - h), n)]
        go(here, here, small_send.at[way, h], small_recv.at[way, h], ring[way])

    def small_lands(way, h):
        here = smalls.at[lax.rem(pos + (h + 1 if way else n - h - 1), n)]
        remote(here, here, small_send.at[way, h], small_recv.at[way, h], ring[way]).wait_recv()

    product(0)
    product(1)
    for load in loads[tiles + 2 :]:
        load.wait()
    turns = {0: [(0, 0)], 1: [(1, 0)], 2: [(0, 1)], 3: [(1, 1)], 4: [(0, 2), (1, 2)], 5: [(2, 0)], 6: [(0, 3), (1, 3)], 7: [(2, 1)]}
    taken = [sum(k == group for some in turns.values() for k, _ in some) for group in range(len(starts))]

    def block(i, _):
        pl.when(i == 4)(functools.partial(product, 2))
        which, part = lax.div(i, 2), lax.rem(i, 2)
        own = lax.rem(which, 2)
        turned = lax.div(which, 2)
        target = lax.rem(next_door + own * (me - next_door) + 2 * (1 - turned), 4)
        at = span(target * tokens + part * half, half)
        total = mm(dz[at, :], wz[...], NT) + mm(d[at, :], w[...], NT)
        work[...] = total

        @pl.when(own == 0)
        def _():
            staged[turned, part] = work[...].astype(bf16)
            near_copy(turned, part).start()

        @pl.when(own == 1)
        def _():
            near_copy(turned, part).wait_recv()

        @pl.when(which == 1)
        def _():
            near[0, part] = (work[...] + near[0, part].astype(f32)).astype(bf16)
            over_copy(part).start()

        @pl.when(which == 3)
        def _():
            near[1, part] = (work[...] + near[1, part].astype(f32)).astype(bf16)

        for at_block, some in turns.items():

            @pl.when(i == at_block)
            def _(some=some):
                for k, h in some:
                    ring_turn(k, h)

        return 0

    lax.fori_loop(0, 8, block, 0)
    for i in range(tiles):
        share = jnp.zeros((tile, LANES), f32)
        for c in range(late // LANES):
            cols = slice(c * LANES, (c + 1) * LANES)
            at = slice(i * tile, (i + 1) * tile)
            share = share + grads[at, cols].astype(f32) * w[at, cols].astype(f32)
        total = mm_exact(jnp.ones((8, LANES), f32), share, NT)[0:1] + gain_ref[0:1, i * tile : (i + 1) * tile]
        for c in range(2 * i, 2 * i + 2):
            row, col = 6 + c // 8, (c % 8) * LANES
            part = total[:, (c - 2 * i) * LANES : (c - 2 * i + 1) * LANES]
            smalls[pos, row : row + 1, col : col + LANES] = part / flat_ref[c : c + 1, :]

    rest = [(k, h) for h in range(n - 1) for k in (2, 0, 1) if h >= taken[k]]
    rest.sort(key=lambda turn: turn[1] - taken[turn[0]])

    def small_step(s):
        for way in (0, 1):
            if s > 0 and (way == 0 or s < n // 2):
                small_lands(way, s - 1)
            if s < n // 2 - way:
                small_hop(way, s)

    small_step(0)
    steps_done = 1
    for at, (k, h) in enumerate(rest):
        ring_turn(k, h)
        if (k, h) == (0, n - 2):
            bc_slot[0] = oxs_ref[:, starts[0][0] : starts[0][0] + 2 * NS]
            go(bc_slot.at[0], bc_slot.at[1], bc_send.at[0], bc_recv.at[0], beside)
        if at % 2 == 1 and steps_done < n // 2:
            small_step(steps_done)
            steps_done += 1
    for s in range(steps_done, n // 2):
        small_step(s)
    small_lands(0, n // 2 - 1)

    total = smalls[0]
    for i in range(1, n):
        total = total + smalls[i]
    tens[me] = total
    others = ((beside, next_door), (across, opposite), (askew, far))
    for k, (peer, _) in enumerate(others):
        go(tens.at[me], tens.at[me], ten_send.at[k], ten_recv.at[k], peer)
    remote(bc_slot.at[1], bc_slot.at[1], bc_send.at[0], bc_recv.at[0], beside).wait_recv()
    bc_slot[2] = bc_slot[0] + bc_slot[1]
    go(bc_slot.at[2], bc_slot.at[3], bc_send.at[1], bc_recv.at[1], across)
    for part in (0, 1):
        over_copy(part).wait_recv()

        def some(i, _, part=part):
            at = span(part * half + i * 32, 32)
            here = span(i * 32, 32)
            oback_ref[at, :] = (near[1, part, here, :].astype(f32) + over[part, here, :].astype(f32)).astype(bf16)
            return 0

        lax.fori_loop(0, half // 32, some, 0)
    for k, (peer, target) in enumerate(others):
        here = tens.at[target]
        remote(here, here, ten_send.at[k], ten_recv.at[k], peer).wait_recv()
    flat_gradients(width, tens, oflat_ref)
    remote(bc_slot.at[3], bc_slot.at[3], bc_send.at[1], bc_recv.at[1], across).wait_recv()
    bc_ref[...] = bc_slot[2] + bc_slot[3]
    for part in (0, 1):
        over_copy(part).wait_send()
        for turned in (0, 1):
            near_copy(turned, part).wait_send()
    for k in range(len(starts)):
        for way in (0, 1):
            for h in range(n - 1):
                hop(k, way, h).wait_send()
    for copy in started:
        copy.wait_send()


def flat_gradients(width, tens, out_ref):
    pairs = width // LANES
    heads = width // P_SIZE

    def sums(row, col):
        total = tens[0, row : row + 1, col : col + LANES]
        for t in range(1, 4):
            total = total + tens[t, row : row + 1, col : col + LANES]
        return total

    def put(row, value):
        out_ref[row : row + 1, :] = value

    for c in range(D // LANES):
        put(c, sums(6 + c // 8, (c % 8) * LANES))
    for t in range(4):
        for c in range(pairs):
            cols = slice(c * LANES, (c + 1) * LANES)
            put(GATE_ROW + pairs * t + c, tens[t, CONV + 1 : CONV + 2, cols])
            put(BIAS_ROW + pairs * t + c, tens[t, CONV : CONV + 1, cols])
            for k in range(CONV):
                put(TAPS_ROW + 4 * pairs * k + pairs * t + c, tens[t, k : k + 1, cols])
    for c in range(2):
        put(BIAS_BC_ROW + c, sums(CONV, width + c * LANES))
        for k in range(CONV):
            put(TAPS_BC_ROW + 2 * k + c, sums(k, width + c * LANES))
    kinds = ((CONV + 1, width), (CONV + 1, width + LANES), (CONV + 3, 512))
    rows = [tens[t, row : row + 1, col : col + LANES] for row, col in kinds for t in range(4)]
    rows = jnp.concatenate(rows + [jnp.zeros((16 - len(rows), LANES), f32)], axis=0)
    lane = lax.broadcasted_iota(jnp.int32, (LANES, 2 * LANES), 1)
    entry = lax.broadcasted_iota(jnp.int32, (LANES, 2 * LANES), 0)
    spread_out = mm_exact(rows, jnp.where(lax.rem(lane, heads) == entry, 1.0, 0.0).astype(f32))
    at = lax.broadcasted_iota(jnp.int32, (16, 2 * LANES), 1)
    source = lax.broadcasted_iota(jnp.int32, (16, 2 * LANES), 0)
    line = jnp.sum(jnp.where(lax.div(at, heads) == source, spread_out, 0.0), axis=0, keepdims=True)
    put(HEAD_ROW, line[:, :LANES])
    put(HEAD_ROW + 1, line[:, LANES:])


def reduce_all(n, xg, d, dz, wp, w, small, flat, gain):
    rows, tokens = D // n, dz.shape[0] // 4
    width, late = dz.shape[1], d.shape[1]
    starts = ((width, late), (0, width // 2), (width // 2, width))
    half = tokens // 2
    dma, vm = pltpu.SemaphoreType.DMA, pltpu.VMEM
    anywhere = pl.BlockSpec(memory_space=pl.ANY)
    inside = pl.BlockSpec(memory_space=pltpu.VMEM)
    return pl.pallas_call(
        functools.partial(reduce_body, n, rows, tokens, starts),
        in_specs=[anywhere] * 6 + [inside] * 2,
        out_specs=[inside] * 4,
        out_shape=[
            jax.ShapeDtypeStruct((rows, late), f32),
            jax.ShapeDtypeStruct((tokens, D), bf16),
            jax.ShapeDtypeStruct((rows, 2 * NS), f32),
            jax.ShapeDtypeStruct((FLAT_ROWS, LANES), f32),
        ],
        scratch_shapes=[
            vm(xg.shape, bf16), vm(d.shape, bf16), vm(dz.shape, bf16), vm((D, width), bf16),
            vm((D, late), bf16),
            vm((half, D), f32), vm((D, late), bf16),
            [[vm((n - 1, size, hi - lo), bf16) for lo, hi in starts] for _, size in cut_rows(rows)],
            vm((2, 2, half, D), bf16), vm((2, 2, half, D), bf16), vm((2, half, D), bf16),
            vm((n, *small.shape), f32), vm((4, *small.shape), f32), vm((4, rows, 2 * NS), f32),
            dma((13,)), dma((2, 3, n - 1)), dma((2, 3, n - 1)), dma((2, 2)), dma((2, 2)), dma((2,)), dma((2,)),
            dma((2, n // 2)), dma((2, n // 2)), dma((3,)), dma((3,)), dma((2,)), dma((2,)),
        ],
        compiler_params=pltpu.CompilerParams(
            collective_id=1, has_side_effects=True, vmem_limit_bytes=46 * 2**20
        ),
        name="reduce_all",
    )(xg, d, dz, wp, w, small, flat, gain)


def adamw_step(weight, first, second, grad, rate, decay):
    first_new = beta_first * first + (1.0 - beta_first) * grad
    second_new = beta_second * second + (1.0 - beta_second) * grad * grad
    hat_first = first_new * (1.0 / (1.0 - beta_first**STEP))
    hat_second = second_new * (1.0 / (1.0 - beta_second**STEP))
    weight_new = weight - rate * (hat_first / (jnp.sqrt(hat_second) + adam_eps) + decay * weight)
    return (weight_new, first_new, second_new)


def finish_body(
    width, heads,
    in_ref, cot_ref, branch_ref, back_ref, flat_ref, early_ref, late_ref, bcg_ref,
    zx_ref, zx1_ref, zx2_ref, bc_ref, bc1_ref, bc2_ref, out_ref, out1_ref, out2_ref, late_all_ref, dt_ref, dt1_ref, dt2_ref,
    layer_ref, grad_ref, zxn_ref, zx1n_ref, zx2n_ref, bcn_ref, bc1n_ref, bc2n_ref,
    outn_ref, out1n_ref, out2n_ref, dtn_ref, dt1n_ref, dt2n_ref,
):
    def update(refs, news, grad):
        fresh = adamw_step(*(ref[...] for ref in refs), grad, matrix_rate, matrix_decay)
        for ref, value in zip(news, fresh):
            ref[...] = value

    for k, grad in ((0, early_ref), (1, late_ref)):
        fresh = adamw_step(
            *(ref[:, k, :] for ref in (zx_ref, zx1_ref, zx2_ref)), grad[:, :width], matrix_rate, matrix_decay
        )
        for ref, value in zip((zxn_ref, zx1n_ref, zx2n_ref), fresh):
            ref[:, k, :] = value
    update((bc_ref, bc1_ref, bc2_ref), (bcn_ref, bc1n_ref, bc2n_ref), bcg_ref[...])
    update((out_ref, out1_ref, out2_ref), (outn_ref, out1n_ref, out2n_ref), early_ref[:, width:])

    @pl.when(pl.program_id(0) == 0)
    def _():
        unit = jnp.where(
            lax.broadcasted_iota(jnp.int32, (16, LANES), 0) == lax.broadcasted_iota(jnp.int32, (16, LANES), 1), 1.0, 0.0
        ).astype(f32)
        turned = mm_exact(unit, late_all_ref[:, width + 2 * NS :], NT)
        update((dt_ref, dt1_ref, dt2_ref), (dtn_ref, dt1n_ref, dt2n_ref), turned[:heads])

    rows = in_ref.shape[0]
    tile = 64

    def some(i, _):
        at = span(i * tile, tile)
        squares = jnp.zeros((tile, LANES), f32)
        inner = jnp.zeros((tile, LANES), f32)
        for c in range(D // LANES):
            cols = slice(c * LANES, (c + 1) * LANES)
            x = in_ref[at, cols].astype(f32)
            squares = squares + x * x
            inner = inner + x * flat_ref[c : c + 1, :] * back_ref[at, cols].astype(f32)
        r = lax.rsqrt(jnp.sum(squares, axis=-1, keepdims=True) / D + norm_eps)
        k = r * r * r * jnp.sum(inner, axis=-1, keepdims=True) / D
        r, k = jnp.broadcast_to(r, (tile, LANES)), jnp.broadcast_to(k, (tile, LANES))
        for c in range(D // LANES):
            cols = slice(c * LANES, (c + 1) * LANES)
            x = in_ref[at, cols].astype(f32)
            layer_ref[at, cols] = (x + branch_ref[at, cols].astype(f32)).astype(bf16)
            back = back_ref[at, cols].astype(f32)
            grad_ref[at, cols] = cot_ref[at, cols].astype(f32) + r * flat_ref[c : c + 1, :] * back - x * k
        return 0

    lax.fori_loop(0, rows // tile, some, 0)


def finish(layer_input, out_grad, branch, back, flat, early, late, bcg, zx, bc, out, dt):
    (rows, width), heads = out[0].shape, dt[0].shape[0]
    steps = 2
    part = lambda a: pl.BlockSpec((a.shape[0] // steps, *a.shape[1:]), lambda i: (i,) + (0,) * (a.ndim - 1))
    whole = lambda a: pl.BlockSpec(a.shape, lambda i: (0,) * a.ndim)
    like = lambda a, dtype=f32: jax.ShapeDtypeStruct(a.shape, dtype)
    weights = (*zx, *bc, *out)
    return pl.pallas_call(
        functools.partial(finish_body, width, heads),
        grid=(steps,),
        in_specs=[
            *(part(a) for a in (layer_input, out_grad, branch, back)), whole(flat),
            *(part(a) for a in (early, late, bcg, *weights)), whole(late), *(whole(a) for a in dt),
        ],
        out_specs=[part(layer_input), part(back), *(part(a) for a in weights), *(whole(a) for a in dt)],
        out_shape=[like(layer_input, bf16), like(layer_input), *(like(a) for a in weights), *(like(a) for a in dt)],
        compiler_params=pltpu.CompilerParams(vmem_limit_bytes=32 * 2**20),
        name="finish",
    )(layer_input, out_grad, branch, back, flat, early, late, bcg, *weights, late, *dt)


def local(
    layer_input,
    out_grad,
    small_params,
    small_first,
    small_second,
    w_zx,
    zx_first,
    zx_second,
    w_bc,
    bc_first,
    bc_second,
    w_dt,
    dt_first,
    dt_second,
    w_out,
    out_first,
    out_second,
):
    n = lax.axis_size("dp")
    flat = jnp.pad(small_params, (0, FLAT_ROWS * LANES - small_params.shape[0])).reshape(FLAT_ROWS, LANES)
    v, xc, dr, st, dy, dz, branch, early, gate, gain, xg, w_all, pair_all, taps, head, chan = ssd_forward(
        n, layer_input, out_grad, flat, w_zx, w_bc, w_dt.T, w_out
    )
    d_late, small, owner_early, own_branch = ssd_backward(
        n, dy, v, xc, dr, st, gate, taps, head, chan, early, branch
    )
    owner_late, d_normed_in, owner_bc, flat_grad = reduce_all(
        n, xg, d_late, dz, pair_all, w_all, small, flat, gain
    )
    small_grad = flat_grad.reshape(-1)[: small_params.shape[0]]
    small_new, small_first_new, small_second_new = adamw_step(
        small_params, small_first, small_second, small_grad, small_rate, 0.0
    )
    (
        layer_output, input_grad, zx_new, zx_first_new, zx_second_new, bc_new, bc_first_new, bc_second_new,
        out_new, out_first_new, out_second_new, dt_new, dt_first_new, dt_second_new,
    ) = finish(
        layer_input, out_grad, own_branch, d_normed_in, flat, owner_early, owner_late, owner_bc,
        (w_zx, zx_first, zx_second), (w_bc, bc_first, bc_second), (w_out, out_first, out_second),
        (w_dt.T, dt_first.T, dt_second.T),
    )
    dt_new, dt_first_new, dt_second_new = dt_new.T, dt_first_new.T, dt_second_new.T
    return (
        layer_output,
        input_grad,
        small_new,
        small_first_new,
        small_second_new,
        zx_new,
        zx_first_new,
        zx_second_new,
        bc_new,
        bc_first_new,
        bc_second_new,
        dt_new,
        dt_first_new,
        dt_second_new,
        out_new,
        out_first_new,
        out_second_new,
    )


def solution(mesh):
    return jax.shard_map(
        local,
        mesh=mesh,
        in_specs=(
            P(("dp", "tensor"), None),
            P(("dp", "tensor"), None),
            P(),
            P(),
            P(),
            P("dp", None, "tensor"),
            P("dp", None, "tensor"),
            P("dp", None, "tensor"),
            P("dp", None),
            P("dp", None),
            P("dp", None),
            P("dp", "tensor"),
            P("dp", "tensor"),
            P("dp", "tensor"),
            P("dp", "tensor"),
            P("dp", "tensor"),
            P("dp", "tensor"),
        ),
        out_specs=(
            P(("dp", "tensor"), None),
            P(("dp", "tensor"), None),
            P(),
            P(),
            P(),
            P("dp", None, "tensor"),
            P("dp", None, "tensor"),
            P("dp", None, "tensor"),
            P("dp", None),
            P("dp", None),
            P("dp", None),
            P("dp", "tensor"),
            P("dp", "tensor"),
            P("dp", "tensor"),
            P("dp", "tensor"),
            P("dp", "tensor"),
            P("dp", "tensor"),
        ),
        check_vma=False,
    )
```

profile of v0, /device:TPU:0, one launch (start us, length us, event | category | flops | bytes accessed | tf_op | source)
XLA Modules:
  0.0 265.4 jit_solution(2728797563093924592)
XLA Ops:
  0.7 1.5 pad_bitcast_fusion.flat_ref
  2.2 133.9 %layer_forward.1 = (bf16[2048,1024]{1,0:T(8,128)(2,1)}, bf16[2048,1024]{1,0:T(8,128)(2,1)}, f32[2048,128]{1,0:T(8,128)}, bf16[16,128,768]{2,1,0:T(8,128)(2,1)}, ...) custom-call(bf16[512,1536]{1,0:T(8,128)(2,1)} %in_ref.3, ...), custom_call_target="tpu_custom_call" | custom-call | tf_op jit(solution)/shard_map/layer_forward/pallas_call | solution.py:679
  136.1 0.0 copy-start.3
  136.1 0.0 copy-start.6
  136.1 0.0 copy-start.16
  136.1 57.2 %layer_backward.1 = (bf16[2048,1152]{1,0:T(8,128)(2,1)}, f32[8,1024]{1,0:T(8,128)}, f32[192,1536]{1,0:T(8,128)}, bf16[512,1536]{1,0:T(8,128)(2,1)}) custom-call(bf16[2048,768]{1,0:T(8,128)(2,1)} %get-tuple-element.55.dy_ref, bf16[2048,1024]{1,0:T(8,128)(2,1)} %get-tuple-element.56.v_ref, bf16[2048,1024]{1,0:T(8,128)(2,1)} %get-tuple-element.57.xc_ref, ...), custom_call_target="tpu_custom_call" | custom-call | tf_op jit(solution)/shard_map/layer_backward/pallas_call | solution.py:1000
  193.4 0.0 copy-done.3
  193.4 0.0 copy-done.6
  193.4 0.0 copy-done.16
  193.4 0.0 copy-start.17
  193.4 0.7 copy-done.17
  194.2 0.0 copy-start.1
  194.2 0.0 copy-start.2
  194.2 0.0 copy-start.4
  194.2 0.0 copy-start.5
  194.2 0.0 copy-start.7
  194.2 0.0 copy-start.8
  194.3 0.0 copy-start.9
  194.3 0.0 copy-start.10
  194.3 0.0 copy-start.11
  194.3 0.0 copy-start.12
  194.3 0.0 copy-start.13
  194.3 0.0 copy-start.14
  194.3 0.0 copy-start.15
  194.3 0.0 copy-start.18
  194.4 0.0 copy-start.19
  194.4 61.5 %reduce_all.1 = (f32[192,1152]{1,0:T(8,128)S(1)}, bf16[512,1536]{1,0:T(8,128)(2,1)S(1)}, f32[192,256]{1,0:T(8,128)S(1)}, f32[168,128]{1,0:T(8,128)S(1)}) custom-call(bf16[2048,1536]{1,0:T(8,128)(2,1)} %get-tuple-element.67.xg_ref, bf16[2048,1152]{1,0:T(8,128)(2,1)} %get-tuple-element.68.d_ref, bf16[2048,768]{1,0:T(8,128)(2,1)S(1)} %copy-done.3, ...), custom_call_target="tpu_custom_call" | custom-call | tf_op jit(solution)/shard_map/reduce_all/pallas_call | solution.py:1309
  255.9 0.0 copy-done.20
  255.9 0.0 copy-done.21
  255.9 0.0 copy-done.22
  255.9 0.7 multiply_subtract_fusion
  256.6 0.0 copy-done
  256.6 0.0 copy-done.1
  256.6 0.0 copy-done.2
  256.6 0.0 copy-done.4
  256.6 0.0 copy-done.5
  256.7 0.0 copy-done.7
  256.7 0.0 copy-done.8
  256.7 0.0 copy-done.9
  256.7 0.0 copy-done.10
  256.7 0.0 copy-done.11
  256.7 0.0 copy-done.12
  256.7 0.0 copy-done.13
  256.7 0.0 copy-done.14
  256.7 0.0 copy-done.15
  256.7 0.0 copy-done.18
  256.8 0.0 copy-done.19
  256.8 8.5 %finish.1 = (bf16[512,1536]{1,0:T(8,128)(2,1)}, f32[512,1536]{1,0:T(8,128)}, f32[192,2,768]{2,1,0:T(2,128)}, f32[192,2,768]{2,1,0:T(2,128)}, f32[192,2,768]{2,1,...) custom-call(bf16[512,1536]{1,0:T(8,128)(2,1)S(1)} %copy-done, ...), custom_call_target="tpu_custom_call" | custom-call | tf_op jit(solution)/shard_map/finish/pallas_call | solution.py:1407
  (4 shorter events, 0.0 us)
Async XLA Ops:
  136.1 57.3 %copy-start.3 = (bf16[2048,768]{1,0:T(8,128)(2,1)S(1)}, bf16[2048,768]{1,0:T(8,128)(2,1)}, u32[]{:S(2)}) copy-start(bf16[2048,768]{1,0:T(8,128)(2,1)} %get-tuple-element.69.dz_ref) | copy-start | bytes 9437188
  136.1 57.3 %copy-start.6 = (f32[168,128]{1,0:T(8,128)S(1)}, f32[168,128]{1,0:T(8,128)}, u32[]{:S(2)}) copy-start(f32[168,128]{1,0:T(8,128)} %pad_bitcast_fusion.flat_ref) | copy-start | bytes 258052
  136.1 57.3 %copy-start.16 = (f32[8,1536]{1,0:T(8,128)S(1)}, f32[8,1536]{1,0:T(8,128)}, u32[]{:S(2)}) copy-start(f32[8,1536]{1,0:T(8,128)} %get-tuple-element.73.gain_ref) | copy-start | bytes 147460
  193.4 0.8 copy-start.17
  194.2 61.7 %copy-start.20 = (f32[21392]{0:T(1024)S(1)}, f32[21392]{0:T(1024)}, u32[]{:S(2)}) copy-start(f32[21392]{0:T(1024)} %param.19) | copy-start | bytes 256708
  194.2 61.7 %copy-start.21 = (f32[21392]{0:T(1024)S(1)}, f32[21392]{0:T(1024)}, u32[]{:S(2)}) copy-start(f32[21392]{0:T(1024)} %param.20) | copy-start | bytes 256708
  194.2 61.7 %copy-start.22 = (f32[21392]{0:T(1024)S(1)}, f32[21392]{0:T(1024)}, u32[]{:S(2)}) copy-start(f32[21392]{0:T(1024)} %param.21) | copy-start | bytes 256708
  194.2 62.4 %copy-start = (bf16[512,1536]{1,0:T(8,128)(2,1)S(1)}, bf16[512,1536]{1,0:T(8,128)(2,1)}, u32[]{:S(2)}) copy-start(bf16[512,1536]{1,0:T(8,128)(2,1)} %in_ref.3) | copy-start | bytes 4718596
  194.2 62.4 %copy-start.1 = (bf16[512,1536]{1,0:T(8,128)(2,1)S(1)}, bf16[512,1536]{1,0:T(8,128)(2,1)}, u32[]{:S(2)}) copy-start(bf16[512,1536]{1,0:T(8,128)(2,1)} %cot_ref.3) | copy-start | bytes 4718596
  194.2 62.4 %copy-start.2 = (f32[192,2,768]{2,1,0:T(2,128)S(1)}, f32[192,2,768]{2,1,0:T(2,128)}, u32[]{:S(2)}) copy-start(f32[192,2,768]{2,1,0:T(2,128)} %zx_ref.1) | copy-start | bytes 3538948
  194.2 62.4 %copy-start.4 = (f32[192,768]{1,0:T(8,128)S(1)}, f32[192,768]{1,0:T(8,128)}, u32[]{:S(2)}) copy-start(f32[192,768]{1,0:T(8,128)} %out_ref.1) | copy-start | bytes 1769476
  194.2 62.4 %copy-start.5 = (bf16[512,1536]{1,0:T(8,128)(2,1)S(1)}, bf16[512,1536]{1,0:T(8,128)(2,1)}, u32[]{:S(2)}) copy-start(bf16[512,1536]{1,0:T(8,128)(2,1)} %get-tuple-element.66.branch_ref) | copy-start | bytes 4718596
  194.2 62.4 %copy-start.7 = (f32[192,2,768]{2,1,0:T(2,128)S(1)}, f32[192,2,768]{2,1,0:T(2,128)}, u32[]{:S(2)}) copy-start(f32[192,2,768]{2,1,0:T(2,128)} %zx1_ref.1) | copy-start | bytes 3538948
  194.2 62.4 %copy-start.8 = (f32[192,2,768]{2,1,0:T(2,128)S(1)}, f32[192,2,768]{2,1,0:T(2,128)}, u32[]{:S(2)}) copy-start(f32[192,2,768]{2,1,0:T(2,128)} %zx2_ref.1) | copy-start | bytes 3538948
  194.3 62.4 %copy-start.9 = (f32[192,1536]{1,0:T(8,128)S(1)}, f32[192,1536]{1,0:T(8,128)}, u32[]{:S(2)}) copy-start(f32[192,1536]{1,0:T(8,128)} %get-tuple-element.75.early_ref) | copy-start | bytes 3538948
  194.3 62.4 %copy-start.10 = (f32[192,256]{1,0:T(8,128)S(1)}, f32[192,256]{1,0:T(8,128)}, u32[]{:S(2)}) copy-start(f32[192,256]{1,0:T(8,128)} %bc_ref.1) | copy-start | bytes 589828
  194.3 62.4 %copy-start.11 = (f32[192,768]{1,0:T(8,128)S(1)}, f32[192,768]{1,0:T(8,128)}, u32[]{:S(2)}) copy-start(f32[192,768]{1,0:T(8,128)} %out1_ref.1) | copy-start | bytes 1769476
  194.3 62.4 %copy-start.12 = (f32[192,768]{1,0:T(8,128)S(1)}, f32[192,768]{1,0:T(8,128)}, u32[]{:S(2)}) copy-start(f32[192,768]{1,0:T(8,128)} %out2_ref.1) | copy-start | bytes 1769476
  194.3 62.4 %copy-start.13 = (f32[192,256]{1,0:T(8,128)S(1)}, f32[192,256]{1,0:T(8,128)}, u32[]{:S(2)}) copy-start(f32[192,256]{1,0:T(8,128)} %bc1_ref.1) | copy-start | bytes 589828
  194.3 62.4 %copy-start.14 = (f32[192,256]{1,0:T(8,128)S(1)}, f32[192,256]{1,0:T(8,128)}, u32[]{:S(2)}) copy-start(f32[192,256]{1,0:T(8,128)} %bc2_ref.1) | copy-start | bytes 589828
  194.3 62.4 %copy-start.15 = (f32[192,12]{0,1:T(8,128)S(1)}, f32[192,12]{0,1:T(8,128)}, u32[]{:S(2)}) copy-start(f32[192,12]{0,1:T(8,128)} %param.28) | copy-start | bytes 27652
  194.3 62.4 %copy-start.18 = (f32[192,12]{0,1:T(8,128)S(1)}, f32[192,12]{0,1:T(8,128)}, u32[]{:S(2)}) copy-start(f32[192,12]{0,1:T(8,128)} %param.29) | copy-start | bytes 27652
  194.4 62.4 %copy-start.19 = (f32[192,12]{0,1:T(8,128)S(1)}, f32[192,12]{0,1:T(8,128)}, u32[]{:S(2)}) copy-start(f32[192,12]{0,1:T(8,128)} %param.30) | copy-start | bytes 27652
where the time goes:
time: 266 us; the launch traced here: 265 us
  Pallas kernels  261 us (98%)
    pallas_call x1, Pallas kernels, ssd_forward(): pl.pallas_call(functools.partial(forward_body, n, rows, tokens, width), g...  134 us
    pallas_call x1, Pallas kernels, reduce_all(): pl.pallas_call(functools.partial(reduce_body, n, rows, tokens, starts), i...  61.5 us
    pallas_call x1, Pallas kernels, ssd_backward(): pl.pallas_call(functools.partial(backward_body, n, own_rows, tokens, widt...  57.2 us
    pallas_call x1, Pallas kernels, finish(): pl.pallas_call(functools.partial(finish_body, width, heads), grid=(steps,...  8.46 us

commit v1 on v0

--- a/solution.py
+++ b/solution.py
@@ -1399,7 +1399,7 @@
 
 def finish(layer_input, out_grad, branch, back, flat, early, late, bcg, zx, bc, out, dt):
     (rows, width), heads = out[0].shape, dt[0].shape[0]
-    steps = 2
+    steps = 4 if rows % 32 == 0 else 2
     part = lambda a: pl.BlockSpec((a.shape[0] // steps, *a.shape[1:]), lambda i: (i,) + (0,) * (a.ndim - 1))
     whole = lambda a: pl.BlockSpec(a.shape, lambda i: (0,) * a.ndim)
     like = lambda a, dtype=f32: jax.ShapeDtypeStruct(a.shape, dtype)

time: 266 us -> 265 us (level)
  no operation moved by 1% of the time
where the time goes in v1:
time: 265 us
  Pallas kernels  260 us (98%)
    pallas_call x1, Pallas kernels, ssd_forward(): pl.pallas_call(functools.partial(forward_body, n, rows, tokens, width), g...  134 us
    pallas_call x1, Pallas kernels, reduce_all(): pl.pallas_call(functools.partial(reduce_body, n, rows, tokens, starts), i...  61.5 us
    pallas_call x1, Pallas kernels, ssd_backward(): pl.pallas_call(functools.partial(backward_body, n, own_rows, tokens, widt...  57.2 us
    pallas_call x1, Pallas kernels, finish(): pl.pallas_call(functools.partial(finish_body, width, heads), grid=(steps,...  7.66 us

profile of v1, /device:TPU:0, one launch (start us, length us, event | category | flops | bytes accessed | tf_op | source)
XLA Modules:
  0.0 264.6 jit_solution(18012125590845726768)
XLA Ops:
  0.7 1.5 pad_bitcast_fusion.flat_ref
  2.2 133.9 %layer_forward.1 = (bf16[2048,1024]{1,0:T(8,128)(2,1)}, bf16[2048,1024]{1,0:T(8,128)(2,1)}, f32[2048,128]{1,0:T(8,128)}, bf16[16,128,768]{2,1,0:T(8,128)(2,1)}, ...) custom-call(bf16[512,1536]{1,0:T(8,128)(2,1)} %in_ref.3, ...), custom_call_target="tpu_custom_call" | custom-call | tf_op jit(solution)/shard_map/layer_forward/pallas_call | solution.py:679
  136.1 0.0 copy-start.3
  136.1 0.0 copy-start.6
  136.1 0.0 copy-start.16
  136.1 57.2 %layer_backward.1 = (bf16[2048,1152]{1,0:T(8,128)(2,1)}, f32[8,1024]{1,0:T(8,128)}, f32[192,1536]{1,0:T(8,128)}, bf16[512,1536]{1,0:T(8,128)(2,1)}) custom-call(bf16[2048,768]{1,0:T(8,128)(2,1)} %get-tuple-element.55.dy_ref, bf16[2048,1024]{1,0:T(8,128)(2,1)} %get-tuple-element.56.v_ref, bf16[2048,1024]{1,0:T(8,128)(2,1)} %get-tuple-element.57.xc_ref, ...), custom_call_target="tpu_custom_call" | custom-call | tf_op jit(solution)/shard_map/layer_backward/pallas_call | solution.py:1000
  193.4 0.0 copy-done.3
  193.4 0.0 copy-done.6
  193.4 0.0 copy-done.16
  193.4 0.0 copy-start.17
  193.4 0.7 copy-done.17
  194.2 0.0 copy-start.1
  194.2 0.0 copy-start.2
  194.2 0.0 copy-start.4
  194.2 0.0 copy-start.5
  194.2 0.0 copy-start.7
  194.2 0.0 copy-start.8
  194.3 0.0 copy-start.9
  194.3 0.0 copy-start.10
  194.3 0.0 copy-start.11
  194.3 0.0 copy-start.12
  194.3 0.0 copy-start.13
  194.3 0.0 copy-start.14
  194.3 0.0 copy-start.15
  194.3 0.0 copy-start.18
  194.4 0.0 copy-start.19
  194.4 61.5 %reduce_all.1 = (f32[192,1152]{1,0:T(8,128)S(1)}, bf16[512,1536]{1,0:T(8,128)(2,1)S(1)}, f32[192,256]{1,0:T(8,128)S(1)}, f32[168,128]{1,0:T(8,128)S(1)}) custom-call(bf16[2048,1536]{1,0:T(8,128)(2,1)} %get-tuple-element.67.xg_ref, bf16[2048,1152]{1,0:T(8,128)(2,1)} %get-tuple-element.68.d_ref, bf16[2048,768]{1,0:T(8,128)(2,1)S(1)} %copy-done.3, ...), custom_call_target="tpu_custom_call" | custom-call | tf_op jit(solution)/shard_map/reduce_all/pallas_call | solution.py:1309
  255.9 0.0 copy-done.20
  255.9 0.0 copy-done.21
  255.9 0.0 copy-done.22
  255.9 0.7 multiply_subtract_fusion
  256.6 0.0 copy-done
  256.6 0.0 copy-done.1
  256.6 0.0 copy-done.2
  256.6 0.0 copy-done.4
  256.6 0.0 copy-done.5
  256.7 0.0 copy-done.7
  256.7 0.0 copy-done.8
  256.7 0.0 copy-done.9
  256.7 0.0 copy-done.10
  256.7 0.0 copy-done.11
  256.7 0.0 copy-done.12
  256.7 0.0 copy-done.13
  256.7 0.0 copy-done.14
  256.7 0.0 copy-done.15
  256.7 0.0 copy-done.18
  256.8 0.0 copy-done.19
  256.8 7.7 %finish.1 = (bf16[512,1536]{1,0:T(8,128)(2,1)}, f32[512,1536]{1,0:T(8,128)}, f32[192,2,768]{2,1,0:T(2,128)}, f32[192,2,768]{2,1,0:T(2,128)}, f32[192,2,768]{2,1,...) custom-call(bf16[512,1536]{1,0:T(8,128)(2,1)S(1)} %copy-done, ...), custom_call_target="tpu_custom_call" | custom-call | tf_op jit(solution)/shard_map/finish/pallas_call | solution.py:1407
  (4 shorter events, 0.0 us)
Async XLA Ops:
  136.1 57.3 %copy-start.3 = (bf16[2048,768]{1,0:T(8,128)(2,1)S(1)}, bf16[2048,768]{1,0:T(8,128)(2,1)}, u32[]{:S(2)}) copy-start(bf16[2048,768]{1,0:T(8,128)(2,1)} %get-tuple-element.69.dz_ref) | copy-start | bytes 9437188
  136.1 57.3 %copy-start.6 = (f32[168,128]{1,0:T(8,128)S(1)}, f32[168,128]{1,0:T(8,128)}, u32[]{:S(2)}) copy-start(f32[168,128]{1,0:T(8,128)} %pad_bitcast_fusion.flat_ref) | copy-start | bytes 258052
  136.1 57.3 %copy-start.16 = (f32[8,1536]{1,0:T(8,128)S(1)}, f32[8,1536]{1,0:T(8,128)}, u32[]{:S(2)}) copy-start(f32[8,1536]{1,0:T(8,128)} %get-tuple-element.73.gain_ref) | copy-start | bytes 147460
  193.4 0.8 copy-start.17
  194.2 61.7 %copy-start.20 = (f32[21392]{0:T(1024)S(1)}, f32[21392]{0:T(1024)}, u32[]{:S(2)}) copy-start(f32[21392]{0:T(1024)} %param.19) | copy-start | bytes 256708
  194.2 61.7 %copy-start.21 = (f32[21392]{0:T(1024)S(1)}, f32[21392]{0:T(1024)}, u32[]{:S(2)}) copy-start(f32[21392]{0:T(1024)} %param.20) | copy-start | bytes 256708
  194.2 61.7 %copy-start.22 = (f32[21392]{0:T(1024)S(1)}, f32[21392]{0:T(1024)}, u32[]{:S(2)}) copy-start(f32[21392]{0:T(1024)} %param.21) | copy-start | bytes 256708
  194.2 62.4 %copy-start = (bf16[512,1536]{1,0:T(8,128)(2,1)S(1)}, bf16[512,1536]{1,0:T(8,128)(2,1)}, u32[]{:S(2)}) copy-start(bf16[512,1536]{1,0:T(8,128)(2,1)} %in_ref.3) | copy-start | bytes 4718596
  194.2 62.4 %copy-start.1 = (bf16[512,1536]{1,0:T(8,128)(2,1)S(1)}, bf16[512,1536]{1,0:T(8,128)(2,1)}, u32[]{:S(2)}) copy-start(bf16[512,1536]{1,0:T(8,128)(2,1)} %cot_ref.3) | copy-start | bytes 4718596
  194.2 62.4 %copy-start.2 = (f32[192,2,768]{2,1,0:T(2,128)S(1)}, f32[192,2,768]{2,1,0:T(2,128)}, u32[]{:S(2)}) copy-start(f32[192,2,768]{2,1,0:T(2,128)} %zx_ref.1) | copy-start | bytes 3538948
  194.2 62.4 %copy-start.4 = (f32[192,768]{1,0:T(8,128)S(1)}, f32[192,768]{1,0:T(8,128)}, u32[]{:S(2)}) copy-start(f32[192,768]{1,0:T(8,128)} %out_ref.1) | copy-start | bytes 1769476
  194.2 62.4 %copy-start.5 = (bf16[512,1536]{1,0:T(8,128)(2,1)S(1)}, bf16[512,1536]{1,0:T(8,128)(2,1)}, u32[]{:S(2)}) copy-start(bf16[512,1536]{1,0:T(8,128)(2,1)} %get-tuple-element.66.branch_ref) | copy-start | bytes 4718596
  194.2 62.4 %copy-start.7 = (f32[192,2,768]{2,1,0:T(2,128)S(1)}, f32[192,2,768]{2,1,0:T(2,128)}, u32[]{:S(2)}) copy-start(f32[192,2,768]{2,1,0:T(2,128)} %zx1_ref.1) | copy-start | bytes 3538948
  194.2 62.4 %copy-start.8 = (f32[192,2,768]{2,1,0:T(2,128)S(1)}, f32[192,2,768]{2,1,0:T(2,128)}, u32[]{:S(2)}) copy-start(f32[192,2,768]{2,1,0:T(2,128)} %zx2_ref.1) | copy-start | bytes 3538948
  194.3 62.4 %copy-start.9 = (f32[192,1536]{1,0:T(8,128)S(1)}, f32[192,1536]{1,0:T(8,128)}, u32[]{:S(2)}) copy-start(f32[192,1536]{1,0:T(8,128)} %get-tuple-element.75.early_ref) | copy-start | bytes 3538948
  194.3 62.4 %copy-start.10 = (f32[192,256]{1,0:T(8,128)S(1)}, f32[192,256]{1,0:T(8,128)}, u32[]{:S(2)}) copy-start(f32[192,256]{1,0:T(8,128)} %bc_ref.1) | copy-start | bytes 589828
  194.3 62.4 %copy-start.11 = (f32[192,768]{1,0:T(8,128)S(1)}, f32[192,768]{1,0:T(8,128)}, u32[]{:S(2)}) copy-start(f32[192,768]{1,0:T(8,128)} %out1_ref.1) | copy-start | bytes 1769476
  194.3 62.4 %copy-start.12 = (f32[192,768]{1,0:T(8,128)S(1)}, f32[192,768]{1,0:T(8,128)}, u32[]{:S(2)}) copy-start(f32[192,768]{1,0:T(8,128)} %out2_ref.1) | copy-start | bytes 1769476
  194.3 62.4 %copy-start.13 = (f32[192,256]{1,0:T(8,128)S(1)}, f32[192,256]{1,0:T(8,128)}, u32[]{:S(2)}) copy-start(f32[192,256]{1,0:T(8,128)} %bc1_ref.1) | copy-start | bytes 589828
  194.3 62.4 %copy-start.14 = (f32[192,256]{1,0:T(8,128)S(1)}, f32[192,256]{1,0:T(8,128)}, u32[]{:S(2)}) copy-start(f32[192,256]{1,0:T(8,128)} %bc2_ref.1) | copy-start | bytes 589828
  194.3 62.4 %copy-start.15 = (f32[192,12]{0,1:T(8,128)S(1)}, f32[192,12]{0,1:T(8,128)}, u32[]{:S(2)}) copy-start(f32[192,12]{0,1:T(8,128)} %param.28) | copy-start | bytes 27652
  194.3 62.4 %copy-start.18 = (f32[192,12]{0,1:T(8,128)S(1)}, f32[192,12]{0,1:T(8,128)}, u32[]{:S(2)}) copy-start(f32[192,12]{0,1:T(8,128)} %param.29) | copy-start | bytes 27652
  194.4 62.4 %copy-start.19 = (f32[192,12]{0,1:T(8,128)S(1)}, f32[192,12]{0,1:T(8,128)}, u32[]{:S(2)}) copy-start(f32[192,12]{0,1:T(8,128)} %param.30) | copy-start | bytes 27652
